TPU v7x, 256 devices: a whole 4x4x8 slice. The times are simulated.
256 devices in a mesh: row: 32 (over z, x), col: 8 (over y, core).
Axes of the slice: x: 4, y: 4, z: 8, core: 2. Of those that a mesh axis runs over, the one named last changes fastest.
Arguments:
- block_cost: bfloat16 [512, 16, 256, 256], P('row', 'col'), may hold values from 0 to 15, as said below
- candidates: int32 [512, 16], P('row', 'col'), may hold values from 0 to 255, all different within a row
- source_logmass: float32 [512, 256], P('row'), may hold values from -4 to 4
- target_logmass: float32 [256, 256], replicated, may hold values from -4 to 4
Outputs:
- source_potential: float32 [512, 256], P('row')
- target_potential: float32 [256, 256], replicated
Inputs may be any that keep to these rules, and one draw needn't show every extreme that they name: Each row of candidates names 16 distinct target blocks, and every target block is named by some row. `block_cost`: costs are nonnegative.
All inputs are finite; a program needn't handle non-finite values.
Results may differ from a plain program's by a relative error of at most 0.0003.
Values sent between devices are 32-bit elements; how exact they have to be, the bound alone decides.
A program may use at most 256 MiB of HBM per device.

v0:
```python
import jax
import jax.numpy as jnp
from jax import lax
from jax.sharding import PartitionSpec as P

ITERS = 2


EPS = 0.05
LOWEST = -1e30


def per_device(block_cost, candidates, source_logmass, target_logmass):
    target_pot = jnp.zeros(target_logmass.shape, jnp.float32)
    source_pot = jnp.zeros(source_logmass.shape, jnp.float32)
    block_size = block_cost.shape[3]
    flat_ids = candidates.reshape(-1)
    for step_index in range(ITERS):
        nearby = target_pot[candidates]
        scores = (nearby[:, :, None, :] - block_cost.astype(jnp.float32)) / EPS
        highest = jnp.max(scores, axis=(1, 3))
        totals = jnp.sum(jnp.exp(scores - highest[:, None, :, None]), axis=(1, 3))
        row_peak = lax.pmax(highest, "col")
        totals = lax.psum(totals * jnp.exp(highest - row_peak), "col")
        highest = row_peak
        source_pot = EPS * source_logmass - EPS * (highest + jnp.log(totals))
        col_scores = (source_pot[:, None, :, None] - block_cost.astype(jnp.float32)) / EPS
        col_high = jnp.max(col_scores, axis=2).reshape(-1, block_size)
        col_total = jnp.sum(
            jnp.exp(col_scores - jnp.max(col_scores, axis=2)[:, :, None, :]), axis=2
        ).reshape(-1, block_size)
        peaks = jnp.full(target_logmass.shape, LOWEST, jnp.float32).at[flat_ids].max(col_high)
        masses = (
            jnp.zeros(target_logmass.shape, jnp.float32)
            .at[flat_ids]
            .add(col_total * jnp.exp(col_high - peaks[flat_ids]))
        )
        all_peaks = lax.pmax(peaks, ("row", "col"))
        masses = lax.psum(masses * jnp.exp(peaks - all_peaks), ("row", "col"))
        target_pot = EPS * target_logmass - EPS * (all_peaks + jnp.log(masses))
    return (source_pot, target_pot)


def solution(mesh):
    return jax.shard_map(
        per_device,
        mesh=mesh,
        in_specs=(P("row", "col", None, None), P("row", "col"), P("row", None), P()),
        out_specs=(P("row", None), P()),
        check_vma=False,
    )
```

profile of v0, /device:TPU:1, one launch (start us, length us, event | category | flops | bytes accessed | tf_op | source)
XLA Modules:
  0.0 1148.2 jit_solution(9444391169057286385)
XLA Ops:
  7.2 0.0 all-reduce.5.cloned.1.call-start
  7.2 0.8 copy.8
  8.0 0.7 compare_select_fusion
  8.6 0.1 copy.9
  8.7 0.1 reshape.62
  8.9 0.6 gather_fusion
  9.5 0.0 copy-start.4
  9.5 3.4 fusion.2
  12.9 23.8 %pmax.28 = f32[16,256]{1,0:T(8,128)S(1)} all-reduce(f32[16,256]{1,0:T(8,128)S(1)} %fusion.2), channel_id=1, replica_groups=mesh['row'=32,'col'=8] {'col'}, use_global_device_ids=true, to_apply=%region_1.0 | all-reduce | flops 4096 | bytes 32768 | tf_op jit(solution)/shard_map/pmax | solution.py:23
  36.7 3.9 fusion.4
  40.6 0.1 reshape.55
  40.7 23.6 %psum.28 = f32[16,256]{1,0:T(8,128)S(1)} all-reduce(f32[16,256]{1,0:T(8,128)S(1)} %exponential_multiply_fusion.3), channel_id=1, replica_groups=mesh['row'=32,'col'=8] {'col'}, use_global_device_ids=true, to_apply=%region_3.0 | all-reduce | flops 4096 | bytes 32768 | tf_op jit(solution)/shard_map/psum | solution.py:24
  64.3 0.0 copy-done.4
  64.3 2.9 fusion.7
  67.2 0.0 copy-start.2
  67.3 1.4 scatter_custom_fusion
  68.7 0.0 copy-start.1
  68.7 0.0 all-reduce.5.cloned.1.call-update
  68.7 0.0 all-reduce.7.cloned.1.call-start
  68.8 3.9 fusion.9
  72.7 0.0 copy-done.1
  72.7 0.9 scatter_custom_fusion.1
  73.7 247.4 %all-reduce.5.cloned.1.call-done = f32[256,256]{1,0:T(8,128)} async-done(((f32[256,256]{1,0:T(8,128)}), f32[256,256]{1,0:T(8,128)}) %all-reduce.5.cloned.1.call-update) | async-done | bytes 262160 | tf_op jit(solution)/shard_map/pmax | solution.py:38
  321.1 1.7 exponential_multiply_fusion.1
  322.8 0.0 all-reduce.7.cloned.1.call-update
  322.8 0.0 all-reduce.9.cloned.1.call-start
  322.9 253.3 %all-reduce.7.cloned.1.call-done = f32[256,256]{1,0:T(8,128)} async-done(((f32[256,256]{1,0:T(8,128)}), f32[256,256]{1,0:T(8,128)}) %all-reduce.7.cloned.1.call-update) | async-done | bytes 262160 | tf_op jit(solution)/shard_map/psum | solution.py:39
  576.2 0.0 copy-done.2
  576.2 1.1 multiply_subtract_fusion.1
  577.3 0.6 gather_fusion.1
  577.9 3.4 fusion.12
  581.3 22.6 %pmax.30 = f32[16,256]{1,0:T(8,128)S(1)} all-reduce(f32[16,256]{1,0:T(8,128)S(1)} %fusion.12), channel_id=1, replica_groups=mesh['row'=32,'col'=8] {'col'}, use_global_device_ids=true, to_apply=%region_11.0 | all-reduce | flops 4096 | bytes 32768 | tf_op jit(solution)/shard_map/pmax | solution.py:23
  603.9 3.9 fusion.14
  607.8 23.6 %psum.30 = f32[16,256]{1,0:T(8,128)S(1)} all-reduce(f32[16,256]{1,0:T(8,128)S(1)} %exponential_multiply_fusion.2), channel_id=1, replica_groups=mesh['row'=32,'col'=8] {'col'}, use_global_device_ids=true, to_apply=%region_13.0 | all-reduce | flops 4096 | bytes 32768 | tf_op jit(solution)/shard_map/psum | solution.py:24
  631.4 0.0 copy-start.3
  631.4 2.9 fusion.17
  634.4 1.4 scatter_custom_fusion.2
  635.8 0.0 copy-start
  635.8 0.0 all-reduce.9.cloned.1.call-update
  635.8 0.0 all-reduce.11.cloned.1.call-start
  635.9 3.9 fusion.19
  639.8 0.0 copy-done.3
  639.8 0.0 copy-done
  639.8 0.9 scatter_custom_fusion.3
  640.8 244.2 %all-reduce.9.cloned.1.call-done = f32[256,256]{1,0:T(8,128)} async-done(((f32[256,256]{1,0:T(8,128)}), f32[256,256]{1,0:T(8,128)}) %all-reduce.9.cloned.1.call-update) | async-done | bytes 262160 | tf_op jit(solution)/shard_map/pmax | solution.py:38
  884.9 1.7 exponential_multiply_fusion
  886.6 0.0 all-reduce.11.cloned.1.call-update
  886.7 253.2 %all-reduce.11.cloned.1.call-done = f32[256,256]{1,0:T(8,128)} async-done(((f32[256,256]{1,0:T(8,128)}), f32[256,256]{1,0:T(8,128)}) %all-reduce.11.cloned.1.call-update) | async-done | bytes 262160 | tf_op jit(solution)/shard_map/psum | solution.py:39
  1139.9 1.8 multiply_subtract_fusion
  (14 shorter events, 0.2 us)
Async XLA Ops:
  7.2 313.9 %all-reduce.5.cloned.1.call-start = ((), (), s32[]{:S(2)}) async-start(), calls=%async_computation | async-start | bytes 524288 | tf_op jit(solution)/shard_map/pmax | solution.py:38
  9.5 54.8 %copy-start.4 = (f32[16,256]{1,0:T(8,128)S(1)}, f32[16,256]{1,0:T(8,128)}, u32[]{:S(2)}) copy-start(f32[16,256]{1,0:T(8,128)} %param.6) | copy-start | bytes 49156
  67.2 509.0 %copy-start.2 = (f32[256,256]{1,0:T(8,128)S(1)}, f32[256,256]{1,0:T(8,128)}, u32[]{:S(2)}) copy-start(f32[256,256]{1,0:T(8,128)} %param.7) | copy-start | bytes 786436
  68.7 4.0 copy-start.1
  68.7 507.5 %all-reduce.7.cloned.1.call-start = ((), (), s32[]{:S(2)}) async-start(), calls=%async_computation.1 | async-start | bytes 524288 | tf_op jit(solution)/shard_map/psum | solution.py:39
  322.8 562.1 %all-reduce.9.cloned.1.call-start = ((), (), s32[]{:S(2)}) async-start(), calls=%async_computation.2 | async-start | bytes 524288 | tf_op jit(solution)/shard_map/pmax | solution.py:38
  631.4 8.4 copy-start.3
  635.8 4.0 copy-start
  635.8 504.0 %all-reduce.11.cloned.1.call-start = ((), (), s32[]{:S(2)}) async-start(), calls=%async_computation.3 | async-start | bytes 524288 | tf_op jit(solution)/shard_map/psum | solution.py:39
Sparse Core Ops, SparseCore 0:
  68.9 252.2 all-reduce.4
  327.1 249.0 all-reduce.6
  636.0 248.9 all-reduce.8
  890.8 249.0 all-reduce.10
where the time goes:
time: 1150 us
  waiting for transfers between devices  998 us (87%)
  blocking collectives  93.5 us (8%)
  other arithmetic  39.9 us (3%)
  between operations  14 us (1%)
    psum x2, waiting for transfers between devices, per_device(): masses = lax.psum(masses * jnp.exp(peaks - all_peaks), ('row', 'col'))  507 us
    pmax x2, waiting for transfers between devices, per_device(): all_peaks = lax.pmax(peaks, ('row', 'col'))  492 us
    psum x2, blocking collectives, per_device(): totals = lax.psum(totals * jnp.exp(highest - row_peak), 'col')  47.1 us
    pmax x2, blocking collectives, per_device(): row_peak = lax.pmax(highest, 'col')  46.4 us
  transfers between devices with their start and end apart: 4, of which 4 were waited for; matrix products, arithmetic and copies ran while one was open for 1% of the time, Pallas kernels for 0%

commit v1 on v0

v1 whole, which is shorter than its diff:
```python
import functools
import math

import jax
import jax.numpy as jnp
from jax import lax
from jax.experimental import pallas as pl
from jax.experimental.pallas import tpu as pltpu
from jax.sharding import PartitionSpec as P

ITERS = 2
EPS = 0.05
LOG2E = math.log2(math.e)
SCALE = LOG2E / EPS
UNSCALE = EPS / LOG2E
LOWEST = -1e30
MESH = pl.DeviceIdType.MESH
NX, NY, NZ, NC = 4, 4, 8, 2
PLANE = NX * NY * NC
NCOL = NY * NC
ROWS, KK, BS = 16, 2, 256
ENT = ROWS * KK
SLAB = 64
GROUP = 8 // KK
HIGHEST = lax.Precision.HIGHEST


def lse2(parts):
    top = jnp.max(parts, axis=0)
    return top + jnp.log2(jnp.sum(jnp.exp2(parts - top[None]), axis=0))


def body(
    cand_ref, cost_hbm, slm_ref, tlm_hbm, src_out, tgt_out,
    cost, c2, tlm, xm, xs, st, ment, sent, onehot, same,
    a_src, a_recv, dense, r_recv, z_src, z_recv, t_src, t_recv,
    in_sem, a_ss, a_rs, r_ss, r_rs, z_ss, z_rs, t_ss, t_rs,
):
    row, col = lax.axis_index("row"), lax.axis_index("col")
    z, x = row // NX, row % NX
    y, co = col // NC, col % NC
    me = x * NCOL + col

    def plane_peer(s):
        px = (x + s // NCOL) % NX
        pc = ((y + (s // NC) % NY) % NY) * NC + (co + s) % NC
        return (z * NX + px, pc), px * NCOL + pc

    def z_peer(s):
        return (((z + s) % NZ) * NX + x, col)

    def in_copy(r):
        return pltpu.make_async_copy(cost_hbm.at[r], cost.at[r], in_sem.at[r])

    def tlm_copy():
        return pltpu.make_async_copy(tlm_hbm.at[pl.ds(me * 8, 8)], tlm, in_sem.at[ROWS])

    def start_in(r, _):
        in_copy(r).start()
        return 0

    lax.fori_loop(0, ROWS, start_in, 0)
    tlm_copy().start()

    barrier = pltpu.get_barrier_semaphore()

    def greet_plane(s, _):
        pl.semaphore_signal(barrier, inc=1, device_id=plane_peer(s)[0], device_id_type=MESH)
        return 0

    def greet_z(s, _):
        pl.semaphore_signal(barrier, inc=1, device_id=z_peer(s), device_id_type=MESH)
        return 0

    lax.fori_loop(1, PLANE, greet_plane, 0)
    lax.fori_loop(1, NZ, greet_z, 0)

    lane = lax.broadcasted_iota(jnp.int32, (BS, 128), 1)
    sub = lax.broadcasted_iota(jnp.int32, (BS, 128), 0)
    sub32 = lax.broadcasted_iota(jnp.int32, (ENT, 128), 0)
    lane32 = lax.broadcasted_iota(jnp.int32, (ENT, 128), 1)
    in_lane = jnp.full((8, 128), -1, jnp.int32)
    in_row = jnp.zeros((ENT, 128), jnp.int32)
    for e in range(ENT):
        c = cand_ref[e % KK, e // KK]
        in_lane = jnp.where(lax.broadcasted_iota(jnp.int32, (8, 128), 1) == e, c, in_lane)
        in_row = jnp.where(sub32 == e, c, in_row)
    lanes32 = jnp.broadcast_to(in_lane[0:1], (ENT, 128))
    equal = jnp.where(in_row == lanes32, 1.0, 0.0)
    same[...] = equal
    earlier = jnp.max(jnp.where(sub32 < lane32, equal, 0.0), axis=0, keepdims=True)
    onehot[...] = jnp.where(
        sub == jnp.broadcast_to(in_lane[0:1], (BS, 128)), 1.0, 0.0
    ) * (1.0 - jnp.broadcast_to(earlier, (BS, 128)))
    missing = jnp.where(jnp.sum(onehot[...], axis=1, keepdims=True) > 0.5, 0.0, LOWEST)

    for step in range(ITERS):
        def source_row(r, _):
            if step == 0:
                in_copy(r).wait()
            mine = lane[:SLAB] == r
            if step > 0:
                shifts, shifts_b = [], []
                for k in range(KK):
                    c = cand_ref[k, r]
                    t = t_recv[step - 1, c // 8, pl.ds(c % 8, 1), :]
                    shifts.append(t)
                    shifts_b.append((t * UNSCALE).astype(jnp.bfloat16))
            for i in range(0, BS, SLAB):
                rows = slice(i, i + SLAB)
                tops = None
                for k in range(KK):
                    for h in (0, 128):
                        v = -cost[r, k, rows, h:h + 128]
                        if step > 0:
                            v = v + shifts_b[k][:, h:h + 128]
                        tops = v if tops is None else jnp.maximum(tops, v)
                top = jnp.max(tops.astype(jnp.float32), axis=1, keepdims=True) * SCALE
                total = None
                for k in range(KK):
                    for h in (0, 128):
                        if step == 0:
                            v = cost[r, k, rows, h:h + 128].astype(jnp.float32) * SCALE
                            c2[r, k, rows, h:h + 128] = v
                            v = -v
                        else:
                            v = shifts[k][:, h:h + 128] - c2[r, k, rows, h:h + 128]
                        p = jnp.exp2(v - top)
                        total = p if total is None else total + p
                total = jnp.sum(total, axis=1, keepdims=True)
                xm[rows, :] = jnp.where(mine, top, xm[rows, :])
                xs[rows, :] = jnp.where(mine, total, xs[rows, :])
            return 0

        lax.fori_loop(0, ROWS, source_row, 0)
        part = xm[...].T[:ROWS] + jnp.log2(xs[...].T[:ROWS])
        a_src[step] = part
        a_recv[step, col] = part
        if step == 0:
            pl.semaphore_wait(barrier, PLANE - 1 + NZ - 1)

        def send_a(s, _):
            pltpu.make_async_remote_copy(
                src_ref=a_src.at[step], dst_ref=a_recv.at[step, col],
                send_sem=a_ss.at[step], recv_sem=a_rs.at[step],
                device_id=plane_peer(s)[0], device_id_type=MESH,
            ).start()
            return 0

        lax.fori_loop(1, NCOL, send_a, 0)
        seven = a_recv.at[step, pl.ds(0, NCOL - 1)]
        pltpu.make_async_copy(seven, seven, a_rs.at[step]).wait()
        source = slm_ref[...] * LOG2E - lse2(a_recv[step])
        if step == ITERS - 1:
            src_out[...] = source * UNSCALE
        st[...] = jnp.concatenate([source, jnp.zeros((128 - ROWS, BS), jnp.float32)], axis=0).T

        def target_row(g, q):
            r = g * GROUP + q
            column = jnp.sum(jnp.where(lane == r, st[...], 0.0), axis=1, keepdims=True)
            wide = jnp.broadcast_to(column, (BS, 128))
            wide_b = (wide * UNSCALE).astype(jnp.bfloat16)
            for k in range(KK):
                for h in (0, 128):
                    v = wide_b - cost[r, k, :, h:h + 128]
                    half = jnp.max(v.reshape(BS // 16, 16, 128), axis=0)
                    top = jnp.max(half.astype(jnp.float32), axis=0, keepdims=True) * SCALE
                    total = None
                    for i in range(0, BS, SLAB):
                        v = (wide[i:i + SLAB] - top) - c2[r, k, i:i + SLAB, h:h + 128]
                        p = jnp.sum(jnp.exp2(v).reshape(SLAB // 8, 8, 128), axis=0)
                        total = p if total is None else total + p
                    total = jnp.sum(total, axis=0, keepdims=True)
                    j = q * KK + k
                    ment[g, j:j + 1, h:h + 128] = top
                    sent[g, j:j + 1, h:h + 128] = total

        def target_rows(g, _):
            for q in range(GROUP):
                target_row(g, q)
            return 0

        lax.fori_loop(0, ROWS // GROUP, target_rows, 0)
        entries = (ment[...] + jnp.log2(sent[...])).reshape(ENT, BS)
        peak = jnp.full((ENT, BS), LOWEST, jnp.float32)
        for e in range(ENT):
            hit = same[:, e:e + 1] > 0.5
            peak = jnp.maximum(peak, jnp.where(hit, entries[e:e + 1], LOWEST))
        mass = jnp.dot(same[:, :ENT], jnp.exp2(entries - peak), precision=HIGHEST,
                       preferred_element_type=jnp.float32)
        merged = peak + jnp.log2(mass)
        spread = jnp.dot(onehot[:, :ENT], merged, precision=HIGHEST,
                         preferred_element_type=jnp.float32) + missing
        dense[step] = spread.reshape(PLANE, 8, BS)
        r_recv[step, me] = dense[step, me]

        def send_r(s, _):
            peer, index = plane_peer(s)
            pltpu.make_async_remote_copy(
                src_ref=dense.at[step, index], dst_ref=r_recv.at[step, me],
                send_sem=r_ss.at[step], recv_sem=r_rs.at[step],
                device_id=peer, device_id_type=MESH,
            ).start()
            return 0

        lax.fori_loop(1, PLANE, send_r, 0)
        others = r_recv.at[step, pl.ds(0, PLANE - 1)]
        pltpu.make_async_copy(others, others, r_rs.at[step]).wait()
        part = lse2(r_recv[step])
        z_src[step] = part
        z_recv[step, z] = part

        def send_z(s, _):
            pltpu.make_async_remote_copy(
                src_ref=z_src.at[step], dst_ref=z_recv.at[step, z],
                send_sem=z_ss.at[step], recv_sem=z_rs.at[step],
                device_id=z_peer(s), device_id_type=MESH,
            ).start()
            return 0

        lax.fori_loop(1, NZ, send_z, 0)
        seven = z_recv.at[step, pl.ds(0, NZ - 1)]
        pltpu.make_async_copy(seven, seven, z_rs.at[step]).wait()
        if step == 0:
            tlm_copy().wait()
        target = tlm[...] * LOG2E - lse2(z_recv[step])
        t_src[step] = target
        t_recv[step, me] = target

        def send_t(s, _):
            pltpu.make_async_remote_copy(
                src_ref=t_src.at[step], dst_ref=t_recv.at[step, me],
                send_sem=t_ss.at[step], recv_sem=t_rs.at[step],
                device_id=plane_peer(s)[0], device_id_type=MESH,
            ).start()
            return 0

        lax.fori_loop(1, PLANE, send_t, 0)
        others = t_recv.at[step, pl.ds(0, PLANE - 1)]
        pltpu.make_async_copy(others, others, t_rs.at[step]).wait()

    tgt_out[...] = t_recv[ITERS - 1]

    for step in range(ITERS):
        for buf, n, sem in (
            (a_recv, NCOL - 1, a_ss), (r_recv, PLANE - 1, r_ss),
            (z_recv, NZ - 1, z_ss), (t_recv, PLANE - 1, t_ss),
        ):
            ref = buf.at[step, pl.ds(0, n)]
            pltpu.make_async_copy(ref, ref, sem.at[step]).wait()


def per_device(block_cost, candidates, source_logmass, target_logmass):
    f32 = jnp.float32
    vmem = pl.BlockSpec(memory_space=pltpu.VMEM)
    dma = pltpu.SemaphoreType.DMA
    source, target = pl.pallas_call(
        body,
        name="sinkhorn",
        out_shape=(
            jax.ShapeDtypeStruct((ROWS, BS), f32),
            jax.ShapeDtypeStruct((PLANE, 8, BS), f32),
        ),
        in_specs=[
            pl.BlockSpec(memory_space=pltpu.SMEM),
            pl.BlockSpec(memory_space=pl.ANY),
            vmem,
            pl.BlockSpec(memory_space=pl.ANY),
        ],
        out_specs=(vmem, vmem),
        scratch_shapes=[
            pltpu.VMEM((ROWS, KK, BS, BS), jnp.bfloat16),
            pltpu.VMEM((ROWS, KK, BS, BS), f32),
            pltpu.VMEM((8, BS), f32),
            pltpu.VMEM((BS, 128), f32),
            pltpu.VMEM((BS, 128), f32),
            pltpu.VMEM((BS, 128), f32),
            pltpu.VMEM((ENT // 8, 8, BS), f32),
            pltpu.VMEM((ENT // 8, 8, BS), f32),
            pltpu.VMEM((BS, 128), f32),
            pltpu.VMEM((ENT, 128), f32),
            pltpu.VMEM((ITERS, ROWS, BS), f32),
            pltpu.VMEM((ITERS, NCOL, ROWS, BS), f32),
            pltpu.VMEM((ITERS, PLANE, 8, BS), f32),
            pltpu.VMEM((ITERS, PLANE, 8, BS), f32),
            pltpu.VMEM((ITERS, 8, BS), f32),
            pltpu.VMEM((ITERS, NZ, 8, BS), f32),
            pltpu.VMEM((ITERS, 8, BS), f32),
            pltpu.VMEM((ITERS, PLANE, 8, BS), f32),
            dma((ROWS + 1,)),
        ] + [dma((ITERS,))] * 8,
        compiler_params=pltpu.CompilerParams(
            collective_id=0, has_side_effects=True, vmem_limit_bytes=60 << 20
        ),
    )(candidates.T, block_cost, source_logmass, target_logmass)
    return source, (target * UNSCALE).reshape(target_logmass.shape)


def solution(mesh):
    return jax.shard_map(
        per_device,
        mesh=mesh,
        in_specs=(P("row", "col", None, None), P("row", "col"), P("row", None), P()),
        out_specs=(P("row", None), P()),
        check_vma=False,
    )
```

time: 1150 us -> 72.6 us (0.06)
  waiting for transfers between devices: 998 us -> 0 us
  blocking collectives: 93.5 us -> 0 us
  Pallas kernels: 0 us -> 68.7 us
  other arithmetic: 39.9 us -> 1.68 us
  between operations: 14 us -> 0.64 us
    psum x2 -> x0, waiting for transfers between devices: 507 us -> none  [per_device(): masses = lax.psum(masses * jnp.exp(peaks - all_peaks), ('row', 'col'))]
    pmax x2 -> x0, waiting for transfers between devices: 492 us -> none  [per_device(): all_peaks = lax.pmax(peaks, ('row', 'col'))]
    pallas_call x0 -> x1, Pallas kernels: none -> 68.7 us  [per_device(): pl.pallas_call(body, name='sinkhorn', out_shape=(jax.ShapeDtypeStruct((RO...]
    psum x2 -> x0, blocking collectives: 47.1 us -> none  [per_device(): totals = lax.psum(totals * jnp.exp(highest - row_peak), 'col')]
    pmax x2 -> x0, blocking collectives: 46.4 us -> none  [per_device(): row_peak = lax.pmax(highest, 'col')]
    reduce_sum x4 -> x0, other arithmetic: 15.6 us -> none  [the longest x2 7.83 us: per_device(): totals = jnp.sum(jnp.exp(scores - highest[:, None, :, None]), axis=(1, 3))]
    reduce_max x4 -> x0, other arithmetic: 12.6 us -> none  [the longest x2 6.72 us: per_device(): highest = jnp.max(scores, axis=(1, 3))]
  transfers between devices with their start and end apart: 4 -> 0, of which waited for: 4 -> 0; matrix products, arithmetic and copies ran while one was open for 1% -> 0% of each run, Pallas kernels for 0% -> 0%
where the time goes in v1:
time: 72.6 us; the launch traced here: 72.3 us
  Pallas kernels  68.7 us (95%)
  other arithmetic  1.68 us (2%)
  local copies, waits for them, and re-layouts  1.32 us (2%)
    pallas_call x1, Pallas kernels, per_device(): pl.pallas_call(body, name='sinkhorn', out_shape=(jax.ShapeDtypeStruct((RO...  68.7 us
    reshape x1, other arithmetic, per_device(): return (source, (target * UNSCALE).reshape(target_logmass.shape))  1.68 us

profile of v1, /device:TPU:1, one launch (start us, length us, event | category | flops | bytes accessed | tf_op | source)
XLA Modules:
  0.0 72.3 jit_solution(11544822693952958100)
XLA Ops:
  0.6 68.7 %sinkhorn.1 = (f32[16,256]{1,0:T(8,128)}, f32[32,8,256]{2,1,0:T(8,128)}) custom-call(s32[2,16]{1,0:T(2,128)} %bitcast.3, bf16[16,2,256,256]{3,2,1,0:T(8,128)(2,1)} %cost_hbm.1, f32[16,256]{1,0:T(8,128)} %slm_ref.1, f32[256,256]{1,0:T(8,128)} %tlm_hbm.1), custom_call_target="tpu_custom_call" | custom-call | tf_op jit(solution)/shard_map/sinkhorn/pallas_call | solution.py:257
  69.3 1.7 %multiply_bitcast_fusion = f32[256,256]{1,0:T(8,128)} fusion(f32[32,8,256]{2,1,0:T(8,128)} %get-tuple-element.5), kind=kLoop, calls=%fused_computation | loop fusion | flops 65536 | bytes 524288 | tf_op jit(solution)/shard_map/reshape | solution.py:296
  71.0 1.3 %copy.7 = f32[16,256]{1,0:T(8,128)} copy(f32[16,256]{1,0:T(8,128)} %get-tuple-element.8) | data formatting | bytes 32768

commit v2 on v0

v2 whole, which is shorter than its diff:
```python
import math

import jax
import jax.numpy as jnp
from jax import lax
from jax.experimental import pallas as pl
from jax.experimental.pallas import tpu as pltpu
from jax.sharding import PartitionSpec as P

ITERS = 2
EPS = 0.05
LOG2E = math.log2(math.e)
SCALE = LOG2E / EPS
UNSCALE = EPS / LOG2E
LOWEST = -1e30
MESH = pl.DeviceIdType.MESH
NX, NY, NZ, NC = 4, 4, 8, 2
PLANE = NX * NY * NC
NCOL = NY * NC
ROWS, KK, BS = 16, 2, 256
ENT = ROWS * KK
HALF = 128
CHUNK = 4
CHUNKS = ROWS // CHUNK
SLAB = 64
F32, BF16 = jnp.float32, jnp.bfloat16


def lse2(parts):
    top = jnp.max(parts, axis=0)
    return top + jnp.log2(jnp.sum(jnp.exp2(parts - top[None]), axis=0))


def body(
    cand_ref, cost_hbm, slm_ref, tlm_hbm, src_out, tgt_out,
    cost, c2, cost_t, c2_t, tlm, slm, spot, st, gath, gath_t, m2, s2,
    ment, sent, named, onehot, missing,
    a_src, a_recv, dense, r_recv, z_src, z_recv, t_src, t_recv00, t_recv01, t_recv10, t_recv11,
    in_sem, a_ss, a_rs, r_ss, r_rs, z_ss, z_rs, t_ss, t_rs,
):
    t_recv = ((t_recv00, t_recv01), (t_recv10, t_recv11))
    row, col = lax.axis_index("row"), lax.axis_index("col")
    z, x = row // NX, row % NX
    y, co = col // NC, col % NC
    me = x * NCOL + col

    def plane_peer(s):
        px = (x + s // NCOL) % NX
        pc = ((y + (s // NC) % NY) % NY) * NC + (co + s) % NC
        return (z * NX + px, pc), px * NCOL + pc

    def z_peer(s):
        return (((z + s) % NZ) * NX + x, col)

    def in_copy(r):
        return pltpu.make_async_copy(cost_hbm.at[r], cost.at[r], in_sem.at[r])

    def tlm_copy():
        return pltpu.make_async_copy(tlm_hbm.at[pl.ds(me * 8, 8)], tlm, in_sem.at[ROWS])

    def start_in(r, _):
        in_copy(r).start()
        return 0

    lax.fori_loop(0, ROWS, start_in, 0)
    tlm_copy().start()

    barrier = pltpu.get_barrier_semaphore()

    def greet_plane(s, _):
        pl.semaphore_signal(barrier, inc=1, device_id=plane_peer(s)[0], device_id_type=MESH)
        return 0

    def greet_z(s, _):
        pl.semaphore_signal(barrier, inc=1, device_id=z_peer(s), device_id_type=MESH)
        return 0

    lax.fori_loop(1, PLANE, greet_plane, 0)
    lax.fori_loop(1, NZ, greet_z, 0)

    def landed(buf, n, sem):
        ref = buf.at[pl.ds(0, n)]
        pltpu.make_async_copy(ref, ref, sem).wait()

    for g in range(CHUNKS):
        slm[g] = slm_ref[g * CHUNK:(g + 1) * CHUNK] * LOG2E

    def cand(e):
        return cand_ref[e % KK, e // KK]

    sub32 = lax.broadcasted_iota(jnp.int32, (ENT, HALF), 0)
    lane32 = lax.broadcasted_iota(jnp.int32, (ENT, HALF), 1)
    lane8 = lax.broadcasted_iota(jnp.int32, (8, HALF), 1)
    in_lane = jnp.full((8, HALF), -1, jnp.int32)
    in_row = jnp.zeros((ENT, HALF), jnp.int32)
    for e in range(ENT):
        c = cand(e)
        in_lane = jnp.where(lane8 % ENT == e, c, in_lane)
        in_row = jnp.where(sub32 == e, c, in_row)
    named[...] = in_row
    earlier = jnp.max(
        jnp.where((sub32 < lane32 % ENT) & (in_row == jnp.broadcast_to(in_lane[0:1], (ENT, HALF))), 1.0, 0.0),
        axis=0, keepdims=True)
    in_lane = jnp.where(lane8 < 3 * ENT, in_lane, -1)[0:1]
    sub = lax.broadcasted_iota(jnp.int32, (BS, HALF), 0)
    hot = jnp.where(sub == jnp.broadcast_to(in_lane, (BS, HALF)), 1.0, 0.0)
    hot = hot * (1.0 - jnp.broadcast_to(earlier, (BS, HALF)))
    onehot[...] = hot.astype(BF16)
    absent = jnp.where(jnp.sum(hot, axis=1, keepdims=True) > 0.5, 0.0, LOWEST)
    missing[...] = jnp.broadcast_to(absent, (BS, HALF))

    lane = lax.broadcasted_iota(jnp.int32, (SLAB, HALF), 1)

    def send_chunk(step, g, part):
        a_src[step, g] = part
        a_recv[step, g, col] = part

        def send(s, _):
            pltpu.make_async_remote_copy(
                src_ref=a_src.at[step, g], dst_ref=a_recv.at[step, g, col],
                send_sem=a_ss.at[step], recv_sem=a_rs.at[step, g],
                device_id=plane_peer(s)[0], device_id_type=MESH,
            ).start()
            return 0

        lax.fori_loop(1, NCOL, send, 0)

    def first_chunk(g):
        for q in range(CHUNK):
            in_copy(g * CHUNK + q).wait()
        packed = []
        for i in range(0, BS, SLAB):
            rows = slice(i, i + SLAB)
            keep = jnp.zeros((SLAB, HALF), F32)
            for q in range(CHUNK):
                r = g * CHUNK + q
                parts = [cost[r, k, rows, h:h + HALF] for k in range(KK) for h in (0, HALF)]
                low = jnp.minimum(jnp.minimum(parts[0], parts[1]), jnp.minimum(parts[2], parts[3]))
                low = jnp.min(low.astype(F32), axis=1, keepdims=True) * SCALE
                total = None
                for p in parts:
                    p = jnp.exp2(low - p.astype(F32) * SCALE)
                    total = p if total is None else total + p
                total = jnp.sum(total, axis=1, keepdims=True)
                keep = jnp.where(lane == q, low, keep)
                keep = jnp.where(lane == CHUNK + q, total, keep)
            packed.append(keep)
        flat = jnp.concatenate(packed, axis=0).T
        return jnp.log2(flat[CHUNK:2 * CHUNK]) - flat[:CHUNK]

    send_chunk(0, 0, first_chunk_after_barrier(first_chunk, barrier))

    def first_rest(g, _):
        send_chunk(0, g, first_chunk(g))
        return 0

    lax.fori_loop(1, CHUNKS, first_rest, 0)

    def scale_costs(r, _):
        for k in range(KK):
            for i in range(0, BS, SLAB):
                c2[r, k, i:i + SLAB] = cost[r, k, i:i + SLAB].astype(F32) * SCALE
        return 0

    lax.fori_loop(0, ROWS, scale_costs, 0)

    def transpose_costs(r, _):
        for k in range(KK):
            turned = cost[r, k].T
            cost_t[r, k] = turned
            c2_t[r, k] = turned.astype(F32) * SCALE
        return 0

    def gather(step, h):
        for e in range(ENT):
            c = cand(e)
            gath[e // 8, e % 8:e % 8 + 1, :] = t_recv[step - 1][h][c // 8, pl.ds(c % 8, 1), :]
        for g in range(CHUNKS):
            gath_t[h, g] = gath[g].T

    def source_half(g, h):
        js = slice(h * HALF, (h + 1) * HALF)
        for q in range(CHUNK):
            r = g * CHUNK + q
            wide = [jnp.broadcast_to(gath_t[h, g, :, q * KK + k:q * KK + k + 1], (HALF, HALF)) for k in range(KK)]
            wide_b = [(w * UNSCALE).astype(BF16) for w in wide]
            for i in (0, HALF):
                top = None
                for k in range(KK):
                    v = wide_b[k] - cost_t[r, k, js, i:i + HALF]
                    v = jnp.max(v.reshape(HALF // 16, 16, HALF), axis=0)
                    top = v if top is None else jnp.maximum(top, v)
                top = jnp.max(top.astype(F32), axis=0, keepdims=True) * SCALE
                total = None
                for k in range(KK):
                    for j in range(0, HALF, SLAB):
                        v = (wide[k][j:j + SLAB] - top) - c2_t[r, k, h * HALF + j:h * HALF + j + SLAB, i:i + HALF]
                        p = jnp.sum(jnp.exp2(v).reshape(SLAB // 8, 8, HALF), axis=0)
                        total = p if total is None else total + p
                m2[h, g, q:q + 1, i:i + HALF] = top
                s2[h, g, q:q + 1, i:i + HALF] = jnp.sum(total, axis=0, keepdims=True)

    def both_halves(g):
        top = jnp.maximum(m2[0, g], m2[1, g])
        total = s2[0, g] * jnp.exp2(m2[0, g] - top) + s2[1, g] * jnp.exp2(m2[1, g] - top)
        return top + jnp.log2(total)

    def take_chunk(step, g):
        landed(a_recv.at[step, g], NCOL - 1, a_rs.at[step, g])
        source = slm[g] - lse2(a_recv[step, g])
        if step == ITERS - 1:
            spot[g] = source * UNSCALE
        st[g] = jnp.concatenate([source, jnp.zeros_like(source)], axis=0).T

    def target_part(g, halves):
        for q in range(CHUNK):
            r = g * CHUNK + q
            wide = jnp.broadcast_to(st[g, :, q:q + 1], (BS, HALF))
            wide_b = (wide * UNSCALE).astype(BF16)
            for k in range(KK):
                for h in halves:
                    js = slice(h * HALF, (h + 1) * HALF)
                    v = wide_b - cost[r, k, :, js]
                    v = jnp.max(v.reshape(BS // 16, 16, HALF), axis=0)
                    top = jnp.max(v.astype(F32), axis=0, keepdims=True) * SCALE
                    total = None
                    for i in range(0, BS, SLAB):
                        v = (wide[i:i + SLAB] - top) - c2[r, k, i:i + SLAB, js]
                        p = jnp.sum(jnp.exp2(v).reshape(SLAB // 8, 8, HALF), axis=0)
                        total = p if total is None else total + p
                    j = q * KK + k
                    ment[h, g, j:j + 1, :] = top
                    sent[h, g, j:j + 1, :] = jnp.sum(total, axis=0, keepdims=True)

    def scatter(step, h):
        entries = (ment[h] + jnp.log2(sent[h])).reshape(ENT, HALF)
        blocks = named[...]
        peak = jnp.full((ENT, HALF), LOWEST, F32)
        for e in range(ENT):
            peak = jnp.maximum(peak, jnp.where(blocks == cand(e), entries[e:e + 1], LOWEST))
        shares = jnp.exp2(entries - peak)
        mass = jnp.zeros((ENT, HALF), F32)
        for e in range(ENT):
            mass = mass + jnp.where(blocks == cand(e), shares[e:e + 1], 0.0)
        merged = peak + jnp.log2(mass)
        first = merged.astype(BF16)
        rest = merged - first.astype(F32)
        second = rest.astype(BF16)
        third = (rest - second.astype(F32)).astype(BF16)
        pieces = jnp.concatenate([first, second, third, jnp.zeros_like(third)], axis=0)
        spread = jnp.dot(onehot[...], pieces, preferred_element_type=F32) + missing[...]
        dense[step, h] = spread.reshape(PLANE, 8, HALF)
        r_recv[step, h, me] = dense[step, h, me]

        def send(s, _):
            peer, index = plane_peer(s)
            pltpu.make_async_remote_copy(
                src_ref=dense.at[step, h, index], dst_ref=r_recv.at[step, h, me],
                send_sem=r_ss.at[step, h], recv_sem=r_rs.at[step, h],
                device_id=peer, device_id_type=MESH,
            ).start()
            return 0

        lax.fori_loop(1, PLANE, send, 0)

    def along_z(step, h):
        landed(r_recv.at[step, h], PLANE - 1, r_rs.at[step, h])
        part = lse2(r_recv[step, h])
        z_src[step, h] = part
        z_recv[step, h, z] = part

        def send(s, _):
            pltpu.make_async_remote_copy(
                src_ref=z_src.at[step, h], dst_ref=z_recv.at[step, h, z],
                send_sem=z_ss.at[step, h], recv_sem=z_rs.at[step, h],
                device_id=z_peer(s), device_id_type=MESH,
            ).start()
            return 0

        lax.fori_loop(1, NZ, send, 0)

    def spread_target(step, h):
        landed(z_recv.at[step, h], NZ - 1, z_rs.at[step, h])
        target = tlm[:, h * HALF:(h + 1) * HALF] * LOG2E - lse2(z_recv[step, h])
        t_src[step, h] = target
        t_recv[step][h][me] = target

        def send(s, _):
            pltpu.make_async_remote_copy(
                src_ref=t_src.at[step, h], dst_ref=t_recv[step][h].at[me],
                send_sem=t_ss.at[step, h], recv_sem=t_rs.at[step, h],
                device_id=plane_peer(s)[0], device_id_type=MESH,
            ).start()
            return 0

        lax.fori_loop(1, PLANE, send, 0)

    for step in range(ITERS):
        if step > 0:
            for h in range(2):
                landed(t_recv[step - 1][h], PLANE - 1, t_rs.at[step - 1, h])
                gather(step, h)

                def source_rows(g, _):
                    source_half(g, h)
                    if h == 1:
                        send_chunk(step, g, both_halves(g))
                    return 0

                lax.fori_loop(0, CHUNKS, source_rows, 0)

        def target_rows(g, _):
            take_chunk(step, g)
            target_part(g, (0, 1))
            return 0

        lax.fori_loop(0, CHUNKS - 1, target_rows, 0)
        take_chunk(step, CHUNKS - 1)
        target_part(CHUNKS - 1, (0,))
        scatter(step, 0)
        target_part(CHUNKS - 1, (1,))
        scatter(step, 1)
        if step == 0:
            tlm_copy().wait()
            lax.fori_loop(0, ROWS // 2, transpose_costs, 0)
        along_z(step, 0)
        along_z(step, 1)
        if step == 0:
            lax.fori_loop(ROWS // 2, ROWS, transpose_costs, 0)
        spread_target(step, 0)
        spread_target(step, 1)

    for g in range(CHUNKS):
        src_out[g * CHUNK:(g + 1) * CHUNK] = spot[g]
    for h in range(2):
        landed(t_recv[ITERS - 1][h], PLANE - 1, t_rs.at[ITERS - 1, h])
        tgt_out[:, h * HALF:(h + 1) * HALF] = t_recv[ITERS - 1][h][...].reshape(PLANE * 8, HALF) * UNSCALE

    for step in range(ITERS):
        ref = a_recv.at[step, :, pl.ds(0, NCOL - 1)]
        pltpu.make_async_copy(ref, ref, a_ss.at[step]).wait()
        for h in range(2):
            landed(r_recv.at[step, h], PLANE - 1, r_ss.at[step, h])
            landed(z_recv.at[step, h], NZ - 1, z_ss.at[step, h])
            landed(t_recv[step][h], PLANE - 1, t_ss.at[step, h])


def first_chunk_after_barrier(first_chunk, barrier):
    part = first_chunk(0)
    pl.semaphore_wait(barrier, PLANE - 1 + NZ - 1)
    return part


def per_device(block_cost, candidates, source_logmass, target_logmass):
    vmem = pl.BlockSpec(memory_space=pltpu.VMEM)
    hbm = pl.BlockSpec(memory_space=pl.ANY)
    dma = pltpu.SemaphoreType.DMA
    scratch = [
        ((ROWS, KK, BS, BS), BF16),
        ((ROWS, KK, BS, BS), F32),
        ((ROWS, KK, BS, BS), BF16),
        ((ROWS, KK, BS, BS), F32),
        ((8, BS), F32),
        ((CHUNKS, CHUNK, BS), F32),
        ((CHUNKS, CHUNK, BS), F32),
        ((CHUNKS, BS, 8), F32),
        ((ENT // 8, 8, HALF), F32),
        ((2, CHUNKS, HALF, 8), F32),
        ((2, CHUNKS, CHUNK, BS), F32),
        ((2, CHUNKS, CHUNK, BS), F32),
        ((2, ENT // 8, 8, HALF), F32),
        ((2, ENT // 8, 8, HALF), F32),
        ((ENT, HALF), jnp.int32),
        ((BS, HALF), BF16),
        ((BS, HALF), F32),
        ((ITERS, CHUNKS, CHUNK, BS), F32),
        ((ITERS, CHUNKS, NCOL, CHUNK, BS), F32),
        ((ITERS, 2, PLANE, 8, HALF), F32),
        ((ITERS, 2, PLANE, 8, HALF), F32),
        ((ITERS, 2, 8, HALF), F32),
        ((ITERS, 2, NZ, 8, HALF), F32),
        ((ITERS, 2, 8, HALF), F32),
    ] + [((PLANE, 8, HALF), F32)] * (2 * ITERS)
    return pl.pallas_call(
        body,
        name="sinkhorn",
        out_shape=(
            jax.ShapeDtypeStruct(source_logmass.shape, F32),
            jax.ShapeDtypeStruct(target_logmass.shape, F32),
        ),
        in_specs=[pl.BlockSpec(memory_space=pltpu.SMEM), hbm, vmem, hbm],
        out_specs=(vmem, vmem),
        scratch_shapes=[pltpu.VMEM(*s) for s in scratch]
        + [dma((ROWS + 1,)), dma((ITERS,)), dma((ITERS, CHUNKS))]
        + [dma((ITERS, 2))] * 6,
        compiler_params=pltpu.CompilerParams(
            collective_id=0, has_side_effects=True, vmem_limit_bytes=60 << 20
        ),
    )(candidates.T, block_cost, source_logmass, target_logmass)


def solution(mesh):
    return jax.shard_map(
        per_device,
        mesh=mesh,
        in_specs=(P("row", "col", None, None), P("row", "col"), P("row", None), P()),
        out_specs=(P("row", None), P()),
        check_vma=False,
    )
```

time: 1150 us -> 68.1 us (0.06)
  waiting for transfers between devices: 998 us -> 0 us
  blocking collectives: 93.5 us -> 0 us
  Pallas kernels: 0 us -> 64.1 us
  other arithmetic: 39.9 us -> 0 us
  between operations: 14 us -> 0.64 us
    psum x2 -> x0, waiting for transfers between devices: 507 us -> none  [per_device(): masses = lax.psum(masses * jnp.exp(peaks - all_peaks), ('row', 'col'))]
    pmax x2 -> x0, waiting for transfers between devices: 492 us -> none  [per_device(): all_peaks = lax.pmax(peaks, ('row', 'col'))]
    pallas_call x0 -> x1, Pallas kernels: none -> 64.1 us  [per_device(): pl.pallas_call(body, name='sinkhorn', out_shape=(jax.ShapeDtypeStruct(sou...]
    psum x2 -> x0, blocking collectives: 47.1 us -> none  [per_device(): totals = lax.psum(totals * jnp.exp(highest - row_peak), 'col')]
    pmax x2 -> x0, blocking collectives: 46.4 us -> none  [per_device(): row_peak = lax.pmax(highest, 'col')]
    reduce_sum x4 -> x0, other arithmetic: 15.6 us -> none  [the longest x2 7.83 us: per_device(): totals = jnp.sum(jnp.exp(scores - highest[:, None, :, None]), axis=(1, 3))]
    reduce_max x4 -> x0, other arithmetic: 12.6 us -> none  [the longest x2 6.72 us: per_device(): highest = jnp.max(scores, axis=(1, 3))]
  transfers between devices with their start and end apart: 4 -> 0, of which waited for: 4 -> 0; matrix products, arithmetic and copies ran while one was open for 1% -> 0% of each run, Pallas kernels for 0% -> 0%
where the time goes in v2:
time: 68.1 us; the launch traced here: 67.8 us
  Pallas kernels  64.1 us (94%)
  local copies, waits for them, and re-layouts  2.99 us (4%)
    pallas_call x1, Pallas kernels, per_device(): pl.pallas_call(body, name='sinkhorn', out_shape=(jax.ShapeDtypeStruct(sou...  64.1 us
    unnamed x2, local copies, waits for them, and re-layouts  2.99 us

profile of v2, /device:TPU:1, one launch (start us, length us, event | category | flops | bytes accessed | tf_op | source)
XLA Modules:
  0.0 67.8 jit_solution(4005208741977486356)
XLA Ops:
  0.6 64.1 %sinkhorn.1 = (f32[16,256]{1,0:T(8,128)}, f32[256,256]{1,0:T(8,128)}) custom-call(s32[2,16]{1,0:T(2,128)} %bitcast.1, bf16[16,2,256,256]{3,2,1,0:T(8,128)(2,1)} %cost_hbm.1, f32[16,256]{1,0:T(8,128)} %slm_ref.1, f32[256,256]{1,0:T(8,128)} %tlm_hbm.1), custom_call_target="tpu_custom_call" | custom-call | tf_op jit(solution)/shard_map/sinkhorn/pallas_call | solution.py:384
  64.8 1.3 %copy.8 = f32[16,256]{1,0:T(8,128)} copy(f32[16,256]{1,0:T(8,128)} %get-tuple-element.4) | data formatting | bytes 32768
  66.1 1.7 %copy.9 = f32[256,256]{1,0:T(8,128)} copy(f32[256,256]{1,0:T(8,128)} %get-tuple-element.5) | data formatting | bytes 524288

commit v3 on v2

--- a/solution.py
+++ b/solution.py
@@ -44,13 +44,28 @@
     y, co = col // NC, col % NC
     me = x * NCOL + col
 
+    def wrap(v, n):
+        return jnp.where(v >= n, v - n, v)
+
+    xs = [wrap(x + d, NX) for d in range(NX)]
+    ys = [wrap(y + d, NY) for d in range(NY)]
+    cs = [co, 1 - co]
+    zrows = [wrap(z + d, NZ) * NX + x for d in range(NZ)]
+    xrows = [z * NX + v for v in xs]
+    cols = [v * NC + c for v in ys for c in cs]
+
+    def hops(s):
+        return min(s // NCOL, NX - s // NCOL) + min(s % NCOL // NC, NY - s % NCOL // NC)
+
+    FAR_PLANE = sorted(range(1, PLANE), key=lambda s: -hops(s))
+    FAR_COL = sorted(range(1, NCOL), key=lambda s: -hops(s))
+    FAR_Z = sorted(range(1, NZ), key=lambda s: -min(s, NZ - s))
+
     def plane_peer(s):
-        px = (x + s // NCOL) % NX
-        pc = ((y + (s // NC) % NY) % NY) * NC + (co + s) % NC
-        return (z * NX + px, pc), px * NCOL + pc
+        return (xrows[s // NCOL], cols[s % NCOL]), xs[s // NCOL] * NCOL + cols[s % NCOL]
 
     def z_peer(s):
-        return (((z + s) % NZ) * NX + x, col)
+        return (zrows[s], col)
 
     def in_copy(r):
         return pltpu.make_async_copy(cost_hbm.at[r], cost.at[r], in_sem.at[r])
@@ -58,103 +73,89 @@
     def tlm_copy():
         return pltpu.make_async_copy(tlm_hbm.at[pl.ds(me * 8, 8)], tlm, in_sem.at[ROWS])
 
-    def start_in(r, _):
+    for r in range(ROWS):
         in_copy(r).start()
-        return 0
-
-    lax.fori_loop(0, ROWS, start_in, 0)
+    barrier = pltpu.get_barrier_semaphore()
+    for s in FAR_Z:
+        pl.semaphore_signal(barrier, inc=1, device_id=z_peer(s), device_id_type=MESH)
+    for s in FAR_PLANE:
+        pl.semaphore_signal(barrier, inc=1, device_id=plane_peer(s)[0], device_id_type=MESH)
     tlm_copy().start()
-
-    barrier = pltpu.get_barrier_semaphore()
-
-    def greet_plane(s, _):
-        pl.semaphore_signal(barrier, inc=1, device_id=plane_peer(s)[0], device_id_type=MESH)
-        return 0
-
-    def greet_z(s, _):
-        pl.semaphore_signal(barrier, inc=1, device_id=z_peer(s), device_id_type=MESH)
-        return 0
-
-    lax.fori_loop(1, PLANE, greet_plane, 0)
-    lax.fori_loop(1, NZ, greet_z, 0)
 
     def landed(buf, n, sem):
         ref = buf.at[pl.ds(0, n)]
         pltpu.make_async_copy(ref, ref, sem).wait()
 
-    for g in range(CHUNKS):
-        slm[g] = slm_ref[g * CHUNK:(g + 1) * CHUNK] * LOG2E
-
     def cand(e):
         return cand_ref[e % KK, e // KK]
 
-    sub32 = lax.broadcasted_iota(jnp.int32, (ENT, HALF), 0)
-    lane32 = lax.broadcasted_iota(jnp.int32, (ENT, HALF), 1)
-    lane8 = lax.broadcasted_iota(jnp.int32, (8, HALF), 1)
-    in_lane = jnp.full((8, HALF), -1, jnp.int32)
-    in_row = jnp.zeros((ENT, HALF), jnp.int32)
-    for e in range(ENT):
-        c = cand(e)
-        in_lane = jnp.where(lane8 % ENT == e, c, in_lane)
-        in_row = jnp.where(sub32 == e, c, in_row)
-    named[...] = in_row
-    earlier = jnp.max(
-        jnp.where((sub32 < lane32 % ENT) & (in_row == jnp.broadcast_to(in_lane[0:1], (ENT, HALF))), 1.0, 0.0),
-        axis=0, keepdims=True)
-    in_lane = jnp.where(lane8 < 3 * ENT, in_lane, -1)[0:1]
-    sub = lax.broadcasted_iota(jnp.int32, (BS, HALF), 0)
-    hot = jnp.where(sub == jnp.broadcast_to(in_lane, (BS, HALF)), 1.0, 0.0)
-    hot = hot * (1.0 - jnp.broadcast_to(earlier, (BS, HALF)))
-    onehot[...] = hot.astype(BF16)
-    absent = jnp.where(jnp.sum(hot, axis=1, keepdims=True) > 0.5, 0.0, LOWEST)
-    missing[...] = jnp.broadcast_to(absent, (BS, HALF))
-
-    lane = lax.broadcasted_iota(jnp.int32, (SLAB, HALF), 1)
-
-    def send_chunk(step, g, part):
+    def tables():
+        for g in range(CHUNKS):
+            slm[g] = slm_ref[g * CHUNK:(g + 1) * CHUNK] * LOG2E
+
+        sub32 = lax.broadcasted_iota(jnp.int32, (ENT, HALF), 0)
+        lane32 = lax.broadcasted_iota(jnp.int32, (ENT, HALF), 1)
+        lane8 = lax.broadcasted_iota(jnp.int32, (8, HALF), 1)
+        in_lane = jnp.full((8, HALF), -1, jnp.int32)
+        in_row = jnp.zeros((ENT, HALF), jnp.int32)
+        for e in range(ENT):
+            c = cand(e)
+            in_lane = jnp.where(lane8 % ENT == e, c, in_lane)
+            in_row = jnp.where(sub32 == e, c, in_row)
+        named[...] = in_row
+        earlier = jnp.max(
+            jnp.where((sub32 < lane32 % ENT) & (in_row == jnp.broadcast_to(in_lane[0:1], (ENT, HALF))), 1.0, 0.0),
+            axis=0, keepdims=True)
+        in_lane = jnp.where(lane8 < 3 * ENT, in_lane, -1)[0:1]
+        sub = lax.broadcasted_iota(jnp.int32, (BS, HALF), 0)
+        hot = jnp.where(sub == jnp.broadcast_to(in_lane, (BS, HALF)), 1.0, 0.0)
+        hot = hot * (1.0 - jnp.broadcast_to(earlier, (BS, HALF)))
+        onehot[...] = hot.astype(BF16)
+        absent = jnp.where(jnp.sum(hot, axis=1, keepdims=True) > 0.5, 0.0, LOWEST)
+        missing[...] = jnp.broadcast_to(absent, (BS, HALF))
+
+    def keep_chunk(step, g, part):
         a_src[step, g] = part
         a_recv[step, g, col] = part
 
-        def send(s, _):
+    def send_chunk(step, g):
+        for s in FAR_COL:
             pltpu.make_async_remote_copy(
                 src_ref=a_src.at[step, g], dst_ref=a_recv.at[step, g, col],
                 send_sem=a_ss.at[step], recv_sem=a_rs.at[step, g],
                 device_id=plane_peer(s)[0], device_id_type=MESH,
             ).start()
-            return 0
-
-        lax.fori_loop(1, NCOL, send, 0)
-
-    def first_chunk(g):
+
+    def first_chunk(g, _):
+        found = []
         for q in range(CHUNK):
             in_copy(g * CHUNK + q).wait()
-        packed = []
-        for i in range(0, BS, SLAB):
-            rows = slice(i, i + SLAB)
-            keep = jnp.zeros((SLAB, HALF), F32)
-            for q in range(CHUNK):
-                r = g * CHUNK + q
-                parts = [cost[r, k, rows, h:h + HALF] for k in range(KK) for h in (0, HALF)]
-                low = jnp.minimum(jnp.minimum(parts[0], parts[1]), jnp.minimum(parts[2], parts[3]))
-                low = jnp.min(low.astype(F32), axis=1, keepdims=True) * SCALE
+        for q in range(CHUNK):
+            r = g * CHUNK + q
+            turned = [cost[r, k].T for k in range(KK)]
+            for k in range(KK):
+                cost_t[r, k] = turned[k]
+            halves = []
+            for i in (0, HALF):
+                low = None
+                for k in range(KK):
+                    v = jnp.min(turned[k][:, i:i + HALF].reshape(BS // 16, 16, HALF), axis=0)
+                    low = v if low is None else jnp.minimum(low, v)
+                low = jnp.min(low.astype(F32), axis=0, keepdims=True) * SCALE
                 total = None
-                for p in parts:
-                    p = jnp.exp2(low - p.astype(F32) * SCALE)
+                for k in range(KK):
+                    p = jnp.exp2(low - turned[k][:, i:i + HALF].astype(F32) * SCALE)
+                    p = jnp.sum(p.reshape(BS // 8, 8, HALF), axis=0)
                     total = p if total is None else total + p
-                total = jnp.sum(total, axis=1, keepdims=True)
-                keep = jnp.where(lane == q, low, keep)
-                keep = jnp.where(lane == CHUNK + q, total, keep)
-            packed.append(keep)
-        flat = jnp.concatenate(packed, axis=0).T
-        return jnp.log2(flat[CHUNK:2 * CHUNK]) - flat[:CHUNK]
-
-    send_chunk(0, 0, first_chunk_after_barrier(first_chunk, barrier))
-
-    def first_rest(g, _):
-        send_chunk(0, g, first_chunk(g))
+                halves.append(jnp.log2(jnp.sum(total, axis=0, keepdims=True)) - low)
+            found.append(jnp.concatenate(halves, axis=1))
+        keep_chunk(0, g, jnp.concatenate(found, axis=0))
         return 0
 
-    lax.fori_loop(1, CHUNKS, first_rest, 0)
+    lax.fori_loop(0, CHUNKS, first_chunk, 0)
+    pl.semaphore_wait(barrier, PLANE - 1 + NZ - 1)
+    for g in range(CHUNKS):
+        send_chunk(0, g)
 
     def scale_costs(r, _):
         for k in range(KK):
@@ -163,12 +164,12 @@
         return 0
 
     lax.fori_loop(0, ROWS, scale_costs, 0)
-
-    def transpose_costs(r, _):
+    tables()
+
+    def scale_turned(r, _):
         for k in range(KK):
-            turned = cost[r, k].T
-            cost_t[r, k] = turned
-            c2_t[r, k] = turned.astype(F32) * SCALE
+            for i in range(0, BS, SLAB):
+                c2_t[r, k, i:i + SLAB] = cost_t[r, k, i:i + SLAB].astype(F32) * SCALE
         return 0
 
     def gather(step, h):
@@ -252,16 +253,13 @@
         dense[step, h] = spread.reshape(PLANE, 8, HALF)
         r_recv[step, h, me] = dense[step, h, me]
 
-        def send(s, _):
+        for s in FAR_PLANE:
             peer, index = plane_peer(s)
             pltpu.make_async_remote_copy(
                 src_ref=dense.at[step, h, index], dst_ref=r_recv.at[step, h, me],
                 send_sem=r_ss.at[step, h], recv_sem=r_rs.at[step, h],
                 device_id=peer, device_id_type=MESH,
             ).start()
-            return 0
-
-        lax.fori_loop(1, PLANE, send, 0)
 
     def along_z(step, h):
         landed(r_recv.at[step, h], PLANE - 1, r_rs.at[step, h])
@@ -269,15 +267,12 @@
         z_src[step, h] = part
         z_recv[step, h, z] = part
 
-        def send(s, _):
+        for s in FAR_Z:
             pltpu.make_async_remote_copy(
                 src_ref=z_src.at[step, h], dst_ref=z_recv.at[step, h, z],
                 send_sem=z_ss.at[step, h], recv_sem=z_rs.at[step, h],
                 device_id=z_peer(s), device_id_type=MESH,
             ).start()
-            return 0
-
-        lax.fori_loop(1, NZ, send, 0)
 
     def spread_target(step, h):
         landed(z_recv.at[step, h], NZ - 1, z_rs.at[step, h])
@@ -285,15 +280,12 @@
         t_src[step, h] = target
         t_recv[step][h][me] = target
 
-        def send(s, _):
+        for s in FAR_PLANE:
             pltpu.make_async_remote_copy(
                 src_ref=t_src.at[step, h], dst_ref=t_recv[step][h].at[me],
                 send_sem=t_ss.at[step, h], recv_sem=t_rs.at[step, h],
                 device_id=plane_peer(s)[0], device_id_type=MESH,
             ).start()
-            return 0
-
-        lax.fori_loop(1, PLANE, send, 0)
 
     for step in range(ITERS):
         if step > 0:
@@ -304,7 +296,8 @@
                 def source_rows(g, _):
                     source_half(g, h)
                     if h == 1:
-                        send_chunk(step, g, both_halves(g))
+                        keep_chunk(step, g, both_halves(g))
+                        send_chunk(step, g)
                     return 0
 
                 lax.fori_loop(0, CHUNKS, source_rows, 0)
@@ -322,11 +315,9 @@
         scatter(step, 1)
         if step == 0:
             tlm_copy().wait()
-            lax.fori_loop(0, ROWS // 2, transpose_costs, 0)
+            lax.fori_loop(0, ROWS, scale_turned, 0)
         along_z(step, 0)
         along_z(step, 1)
-        if step == 0:
-            lax.fori_loop(ROWS // 2, ROWS, transpose_costs, 0)
         spread_target(step, 0)
         spread_target(step, 1)
 
@@ -343,12 +334,6 @@
             landed(r_recv.at[step, h], PLANE - 1, r_ss.at[step, h])
             landed(z_recv.at[step, h], NZ - 1, z_ss.at[step, h])
             landed(t_recv[step][h], PLANE - 1, t_ss.at[step, h])
-
-
-def first_chunk_after_barrier(first_chunk, barrier):
-    part = first_chunk(0)
-    pl.semaphore_wait(barrier, PLANE - 1 + NZ - 1)
-    return part
 
 
 def per_device(block_cost, candidates, source_logmass, target_logmass):

time: 68.1 us -> 62.3 us (0.915)
  Pallas kernels: 64.1 us -> 58.4 us
    pallas_call x1, Pallas kernels: 64.1 us -> 58.4 us  [per_device(): pl.pallas_call(body, name='sinkhorn', out_shape=(jax.ShapeDtypeStruct(sou...]
where the time goes in v3:
time: 62.3 us; the launch traced here: 62.1 us
  Pallas kernels  58.4 us (94%)
  local copies, waits for them, and re-layouts  2.99 us (5%)
  between operations  0.64 us (1%)
    pallas_call x1, Pallas kernels, per_device(): pl.pallas_call(body, name='sinkhorn', out_shape=(jax.ShapeDtypeStruct(sou...  58.4 us
    unnamed x2, local copies, waits for them, and re-layouts  2.99 us

profile of v3, /device:TPU:1, one launch (start us, length us, event | category | flops | bytes accessed | tf_op | source)
XLA Modules:
  0.0 62.1 jit_solution(14281454544843517613)
XLA Ops:
  0.6 58.4 %sinkhorn.1 = (f32[16,256]{1,0:T(8,128)}, f32[256,256]{1,0:T(8,128)}) custom-call(s32[2,16]{1,0:T(2,128)} %bitcast.1, bf16[16,2,256,256]{3,2,1,0:T(8,128)(2,1)} %cost_hbm.1, f32[16,256]{1,0:T(8,128)} %slm_ref.1, f32[256,256]{1,0:T(8,128)} %tlm_hbm.1), custom_call_target="tpu_custom_call" | custom-call | tf_op jit(solution)/shard_map/sinkhorn/pallas_call | solution.py:369
  59.1 1.3 %copy.8 = f32[16,256]{1,0:T(8,128)} copy(f32[16,256]{1,0:T(8,128)} %get-tuple-element.4) | data formatting | bytes 32768
  60.4 1.7 %copy.9 = f32[256,256]{1,0:T(8,128)} copy(f32[256,256]{1,0:T(8,128)} %get-tuple-element.5) | data formatting | bytes 524288

commit v4 on v3

--- a/solution.py
+++ b/solution.py
@@ -23,6 +23,7 @@
 CHUNK = 4
 CHUNKS = ROWS // CHUNK
 SLAB = 64
+PIECES = 4
 F32, BF16 = jnp.float32, jnp.bfloat16
 
 
@@ -126,36 +127,44 @@
                 device_id=plane_peer(s)[0], device_id_type=MESH,
             ).start()
 
-    def first_chunk(g, _):
+    def first_chunk(g):
         found = []
         for q in range(CHUNK):
-            in_copy(g * CHUNK + q).wait()
-        for q in range(CHUNK):
             r = g * CHUNK + q
-            turned = [cost[r, k].T for k in range(KK)]
-            for k in range(KK):
-                cost_t[r, k] = turned[k]
+            in_copy(r).wait()
             halves = []
             for i in (0, HALF):
+                turned = [cost[r, k, i:i + HALF, :].T for k in range(KK)]
                 low = None
                 for k in range(KK):
-                    v = jnp.min(turned[k][:, i:i + HALF].reshape(BS // 16, 16, HALF), axis=0)
+                    cost_t[r, k, :, i:i + HALF] = turned[k]
+                    v = jnp.min(turned[k].reshape(BS // 16, 16, HALF), axis=0)
                     low = v if low is None else jnp.minimum(low, v)
                 low = jnp.min(low.astype(F32), axis=0, keepdims=True) * SCALE
                 total = None
                 for k in range(KK):
-                    p = jnp.exp2(low - turned[k][:, i:i + HALF].astype(F32) * SCALE)
+                    p = jnp.exp2(low - turned[k].astype(F32) * SCALE)
                     p = jnp.sum(p.reshape(BS // 8, 8, HALF), axis=0)
                     total = p if total is None else total + p
                 halves.append(jnp.log2(jnp.sum(total, axis=0, keepdims=True)) - low)
             found.append(jnp.concatenate(halves, axis=1))
         keep_chunk(0, g, jnp.concatenate(found, axis=0))
+
+    def first_rows(g, _):
+        first_chunk(g)
         return 0
 
-    lax.fori_loop(0, CHUNKS, first_chunk, 0)
+    def first_rows_sent(g, _):
+        first_chunk(g)
+        send_chunk(0, g)
+        return 0
+
+    tables()
+    lax.fori_loop(0, 2, first_rows, 0)
     pl.semaphore_wait(barrier, PLANE - 1 + NZ - 1)
-    for g in range(CHUNKS):
-        send_chunk(0, g)
+    send_chunk(0, 0)
+    send_chunk(0, 1)
+    lax.fori_loop(2, CHUNKS, first_rows_sent, 0)
 
     def scale_costs(r, _):
         for k in range(KK):
@@ -164,7 +173,6 @@
         return 0
 
     lax.fori_loop(0, ROWS, scale_costs, 0)
-    tables()
 
     def scale_turned(r, _):
         for k in range(KK):
@@ -334,6 +342,23 @@
             landed(r_recv.at[step, h], PLANE - 1, r_ss.at[step, h])
             landed(z_recv.at[step, h], NZ - 1, z_ss.at[step, h])
             landed(t_recv[step][h], PLANE - 1, t_ss.at[step, h])
+
+
+def hand_over(source, target, src_out, tgt_out, held_s, held_t, in_sem, out_sem):
+    ways = [(source, held_s, src_out)]
+    size = target.shape[0] // PIECES
+    for i in range(PIECES):
+        part = pl.ds(i * size, size)
+        ways.append((target.at[part], held_t.at[part], tgt_out.at[part]))
+    ins = [pltpu.make_async_copy(a, v, in_sem.at[i]) for i, (a, v, _) in enumerate(ways)]
+    outs = [pltpu.make_async_copy(v, b, out_sem.at[i]) for i, (_, v, b) in enumerate(ways)]
+    for c in ins:
+        c.start()
+    for c, d in zip(ins, outs):
+        c.wait()
+        d.start()
+    for d in outs:
+        d.wait()
 
 
 def per_device(block_cost, candidates, source_logmass, target_logmass):
@@ -366,7 +391,7 @@
         ((ITERS, 2, NZ, 8, HALF), F32),
         ((ITERS, 2, 8, HALF), F32),
     ] + [((PLANE, 8, HALF), F32)] * (2 * ITERS)
-    return pl.pallas_call(
+    source, target = pl.pallas_call(
         body,
         name="sinkhorn",
         out_shape=(
@@ -382,6 +407,22 @@
             collective_id=0, has_side_effects=True, vmem_limit_bytes=60 << 20
         ),
     )(candidates.T, block_cost, source_logmass, target_logmass)
+    return pl.pallas_call(
+        hand_over,
+        name="hand_over",
+        out_shape=(
+            jax.ShapeDtypeStruct(source_logmass.shape, F32),
+            jax.ShapeDtypeStruct(target_logmass.shape, F32),
+        ),
+        in_specs=[hbm, hbm],
+        out_specs=(hbm, hbm),
+        scratch_shapes=[
+            pltpu.VMEM(source_logmass.shape, F32),
+            pltpu.VMEM(target_logmass.shape, F32),
+            dma((PIECES + 1,)),
+            dma((PIECES + 1,)),
+        ],
+    )(source, target)
 
 
 def solution(mesh):

time: 62.3 us -> 61.2 us (0.982)
  local copies, waits for them, and re-layouts: 2.99 us -> 0 us
  Pallas kernels: 58.4 us -> 60.3 us
    unnamed x2 -> x0, local copies, waits for them, and re-layouts: 2.99 us -> none
    pallas_call x0 -> x1, Pallas kernels: none -> 1.67 us  [per_device(): pl.pallas_call(hand_over, name='hand_over', out_shape=(jax.ShapeDtypeStru...]
where the time goes in v4:
time: 61.2 us; the launch traced here: 60.9 us
  Pallas kernels  60.3 us (99%)
  between operations  0.64 us (1%)
    pallas_call x1, Pallas kernels, per_device(): pl.pallas_call(body, name='sinkhorn', out_shape=(jax.ShapeDtypeStruct(sou...  58.6 us
    pallas_call x1, Pallas kernels, per_device(): pl.pallas_call(hand_over, name='hand_over', out_shape=(jax.ShapeDtypeStru...  1.67 us

profile of v4, /device:TPU:1, one launch (start us, length us, event | category | flops | bytes accessed | tf_op | source)
XLA Modules:
  0.0 60.9 jit_solution(14356543454969734818)
XLA Ops:
  0.6 58.6 %sinkhorn.1 = (f32[16,256]{1,0:T(8,128)}, f32[256,256]{1,0:T(8,128)}) custom-call(s32[2,16]{1,0:T(2,128)} %bitcast.1, bf16[16,2,256,256]{3,2,1,0:T(8,128)(2,1)} %cost_hbm.1, f32[16,256]{1,0:T(8,128)} %slm_ref.1, f32[256,256]{1,0:T(8,128)} %tlm_hbm.1), custom_call_target="tpu_custom_call" | custom-call | tf_op jit(solution)/shard_map/sinkhorn/pallas_call | solution.py:394
  59.2 1.7 %hand_over.1 = (f32[16,256]{1,0:T(8,128)}, f32[256,256]{1,0:T(8,128)}) custom-call(f32[16,256]{1,0:T(8,128)} %get-tuple-element.4.source, f32[256,256]{1,0:T(8,128)} %get-tuple-element.5.target), custom_call_target="tpu_custom_call" | custom-call | tf_op jit(solution)/shard_map/hand_over/pallas_call | solution.py:410

commit v5 on v4

--- a/solution.py
+++ b/solution.py
@@ -34,12 +34,12 @@
 
 def body(
     cand_ref, cost_hbm, slm_ref, tlm_hbm, src_out, tgt_out,
-    cost, c2, cost_t, c2_t, tlm, slm, spot, st, gath, gath_t, m2, s2,
+    cost, c2, cost_t, c2_t, tlm, slm, spot, held, st, gath, gath_t, m2, s2,
     ment, sent, named, onehot, missing,
-    a_src, a_recv, dense, r_recv, z_src, z_recv, t_src, t_recv00, t_recv01, t_recv10, t_recv11,
-    in_sem, a_ss, a_rs, r_ss, r_rs, z_ss, z_rs, t_ss, t_rs,
+    a_src, a_recv, dense, r_recv, z_src, z_recv, t_src, t_recv0, t_recv1,
+    in_sem, out_sem, a_ss, a_rs, r_ss, r_rs, z_ss, z_rs, t_ss, t_rs,
 ):
-    t_recv = ((t_recv00, t_recv01), (t_recv10, t_recv11))
+    t_recv = ((t_recv0, t_recv1), (tgt_out.at[0], tgt_out.at[1]))
     row, col = lax.axis_index("row"), lax.axis_index("col")
     z, x = row // NX, row % NX
     y, co = col // NC, col % NC
@@ -130,8 +130,9 @@
     def first_chunk(g):
         found = []
         for q in range(CHUNK):
+            in_copy(g * CHUNK + q).wait()
+        for q in range(CHUNK):
             r = g * CHUNK + q
-            in_copy(r).wait()
             halves = []
             for i in (0, HALF):
                 turned = [cost[r, k, i:i + HALF, :].T for k in range(KK)]
@@ -282,11 +283,21 @@
                 device_id=z_peer(s), device_id_type=MESH,
             ).start()
 
+    def own_copy(h):
+        return pltpu.make_async_copy(t_src.at[ITERS - 1, h], tgt_out.at[h, me], out_sem.at[h])
+
+    def source_copy():
+        return pltpu.make_async_copy(held, src_out, out_sem.at[2])
+
     def spread_target(step, h):
         landed(z_recv.at[step, h], NZ - 1, z_rs.at[step, h])
         target = tlm[:, h * HALF:(h + 1) * HALF] * LOG2E - lse2(z_recv[step, h])
-        t_src[step, h] = target
-        t_recv[step][h][me] = target
+        if step < ITERS - 1:
+            t_src[step, h] = target
+            t_recv[step][h][me] = target
+        else:
+            t_src[step, h] = target * UNSCALE
+            own_copy(h).start()
 
         for s in FAR_PLANE:
             pltpu.make_async_remote_copy(
@@ -324,16 +335,19 @@
         if step == 0:
             tlm_copy().wait()
             lax.fori_loop(0, ROWS, scale_turned, 0)
+        if step == ITERS - 1:
+            for g in range(CHUNKS):
+                held[g * CHUNK:(g + 1) * CHUNK] = spot[g]
+            source_copy().start()
         along_z(step, 0)
         along_z(step, 1)
         spread_target(step, 0)
         spread_target(step, 1)
 
-    for g in range(CHUNKS):
-        src_out[g * CHUNK:(g + 1) * CHUNK] = spot[g]
     for h in range(2):
         landed(t_recv[ITERS - 1][h], PLANE - 1, t_rs.at[ITERS - 1, h])
-        tgt_out[:, h * HALF:(h + 1) * HALF] = t_recv[ITERS - 1][h][...].reshape(PLANE * 8, HALF) * UNSCALE
+        own_copy(h).wait()
+    source_copy().wait()
 
     for step in range(ITERS):
         ref = a_recv.at[step, :, pl.ds(0, NCOL - 1)]
@@ -346,10 +360,13 @@
 
 def hand_over(source, target, src_out, tgt_out, held_s, held_t, in_sem, out_sem):
     ways = [(source, held_s, src_out)]
-    size = target.shape[0] // PIECES
+    size = tgt_out.shape[0] * 2 // PIECES
     for i in range(PIECES):
-        part = pl.ds(i * size, size)
-        ways.append((target.at[part], held_t.at[part], tgt_out.at[part]))
+        h, first = i % 2, i // 2 * size
+        part = pl.ds(first, size)
+        ways.append((
+            target.at[h, part], held_t.at[h, part], tgt_out.at[part, pl.ds(h * HALF, HALF)]
+        ))
     ins = [pltpu.make_async_copy(a, v, in_sem.at[i]) for i, (a, v, _) in enumerate(ways)]
     outs = [pltpu.make_async_copy(v, b, out_sem.at[i]) for i, (_, v, b) in enumerate(ways)]
     for c in ins:
@@ -373,6 +390,7 @@
         ((8, BS), F32),
         ((CHUNKS, CHUNK, BS), F32),
         ((CHUNKS, CHUNK, BS), F32),
+        ((ROWS, BS), F32),
         ((CHUNKS, BS, 8), F32),
         ((ENT // 8, 8, HALF), F32),
         ((2, CHUNKS, HALF, 8), F32),
@@ -390,18 +408,18 @@
         ((ITERS, 2, 8, HALF), F32),
         ((ITERS, 2, NZ, 8, HALF), F32),
         ((ITERS, 2, 8, HALF), F32),
-    ] + [((PLANE, 8, HALF), F32)] * (2 * ITERS)
+    ] + [((PLANE, 8, HALF), F32)] * 2
     source, target = pl.pallas_call(
         body,
         name="sinkhorn",
         out_shape=(
             jax.ShapeDtypeStruct(source_logmass.shape, F32),
-            jax.ShapeDtypeStruct(target_logmass.shape, F32),
+            jax.ShapeDtypeStruct((2, PLANE, 8, HALF), F32),
         ),
         in_specs=[pl.BlockSpec(memory_space=pltpu.SMEM), hbm, vmem, hbm],
-        out_specs=(vmem, vmem),
+        out_specs=(hbm, hbm),
         scratch_shapes=[pltpu.VMEM(*s) for s in scratch]
-        + [dma((ROWS + 1,)), dma((ITERS,)), dma((ITERS, CHUNKS))]
+        + [dma((ROWS + 1,)), dma((3,)), dma((ITERS,)), dma((ITERS, CHUNKS))]
         + [dma((ITERS, 2))] * 6,
         compiler_params=pltpu.CompilerParams(
             collective_id=0, has_side_effects=True, vmem_limit_bytes=60 << 20
@@ -418,11 +436,11 @@
         out_specs=(hbm, hbm),
         scratch_shapes=[
             pltpu.VMEM(source_logmass.shape, F32),
-            pltpu.VMEM(target_logmass.shape, F32),
+            pltpu.VMEM((2, PLANE * 8, HALF), F32),
             dma((PIECES + 1,)),
             dma((PIECES + 1,)),
         ],
-    )(source, target)
+    )(source, target.reshape(2, PLANE * 8, HALF))
 
 
 def solution(mesh):

time: 61.2 us -> 60.5 us (0.989)
  Pallas kernels: 60.3 us -> 59.5 us
    pallas_call x1, Pallas kernels: 58.6 us -> 57.9 us  [per_device(): pl.pallas_call(body, name='sinkhorn', out_shape=(jax.ShapeDtypeStruct(sou...]
where the time goes in v5:
time: 60.5 us; the launch traced here: 60.2 us
  Pallas kernels  59.5 us (98%)
  between operations  0.64 us (1%)
    pallas_call x1, Pallas kernels, per_device(): pl.pallas_call(body, name='sinkhorn', out_shape=(jax.ShapeDtypeStruct(sou...  57.9 us
    pallas_call x1, Pallas kernels, per_device(): pl.pallas_call(hand_over, name='hand_over', out_shape=(jax.ShapeDtypeStru...  1.67 us

profile of v5, /device:TPU:1, one launch (start us, length us, event | category | flops | bytes accessed | tf_op | source)
XLA Modules:
  0.0 60.2 jit_solution(8642122790982535432)
XLA Ops:
  0.6 57.9 %sinkhorn.1 = (f32[16,256]{1,0:T(8,128)}, f32[2,32,8,128]{3,2,1,0:T(8,128)}) custom-call(s32[2,16]{1,0:T(2,128)} %bitcast.3, bf16[16,2,256,256]{3,2,1,0:T(8,128)(2,1)} %cost_hbm.1, f32[16,256]{1,0:T(8,128)} %slm_ref.1, f32[256,256]{1,0:T(8,128)} %tlm_hbm.1), custom_call_target="tpu_custom_call" | custom-call | tf_op jit(solution)/shard_map/sinkhorn/pallas_call | solution.py:412
  58.5 1.7 %hand_over.1 = (f32[16,256]{1,0:T(8,128)}, f32[256,256]{1,0:T(8,128)}) custom-call(f32[16,256]{1,0:T(8,128)} %get-tuple-element.4.source, f32[2,256,128]{2,1,0:T(8,128)} %bitcast.2), custom_call_target="tpu_custom_call" | custom-call | tf_op jit(solution)/shard_map/hand_over/pallas_call | solution.py:428

commit v6 on v5

--- a/solution.py
+++ b/solution.py
@@ -321,16 +321,20 @@
 
                 lax.fori_loop(0, CHUNKS, source_rows, 0)
 
-        def target_rows(g, _):
-            take_chunk(step, g)
-            target_part(g, (0, 1))
+        def target_rows_first(g, _):
+            take_chunk(step, g + 1)
+            target_part(g, (0,))
             return 0
 
-        lax.fori_loop(0, CHUNKS - 1, target_rows, 0)
-        take_chunk(step, CHUNKS - 1)
+        def target_rows_second(g, _):
+            target_part(g, (1,))
+            return 0
+
+        take_chunk(step, 0)
+        lax.fori_loop(0, CHUNKS - 1, target_rows_first, 0)
         target_part(CHUNKS - 1, (0,))
         scatter(step, 0)
-        target_part(CHUNKS - 1, (1,))
+        lax.fori_loop(0, CHUNKS, target_rows_second, 0)
         scatter(step, 1)
         if step == 0:
             tlm_copy().wait()

time: 60.5 us -> 59.3 us (0.980)
  Pallas kernels: 59.5 us -> 58.3 us
    pallas_call x1, Pallas kernels: 57.9 us -> 56.6 us  [per_device(): pl.pallas_call(body, name='sinkhorn', out_shape=(jax.ShapeDtypeStruct(sou...]
where the time goes in v6:
time: 59.3 us; the launch traced here: 59 us
  Pallas kernels  58.3 us (98%)
  between operations  0.64 us (1%)
    pallas_call x1, Pallas kernels, per_device(): pl.pallas_call(body, name='sinkhorn', out_shape=(jax.ShapeDtypeStruct(sou...  56.6 us
    pallas_call x1, Pallas kernels, per_device(): pl.pallas_call(hand_over, name='hand_over', out_shape=(jax.ShapeDtypeStru...  1.67 us

profile of v6, /device:TPU:1, one launch (start us, length us, event | category | flops | bytes accessed | tf_op | source)
XLA Modules:
  0.0 59.0 jit_solution(17404103711181431386)
XLA Ops:
  0.6 56.6 %sinkhorn.1 = (f32[16,256]{1,0:T(8,128)}, f32[2,32,8,128]{3,2,1,0:T(8,128)}) custom-call(s32[2,16]{1,0:T(2,128)} %bitcast.3, bf16[16,2,256,256]{3,2,1,0:T(8,128)(2,1)} %cost_hbm.1, f32[16,256]{1,0:T(8,128)} %slm_ref.1, f32[256,256]{1,0:T(8,128)} %tlm_hbm.1), custom_call_target="tpu_custom_call" | custom-call | tf_op jit(solution)/shard_map/sinkhorn/pallas_call | solution.py:416
  57.3 1.7 %hand_over.1 = (f32[16,256]{1,0:T(8,128)}, f32[256,256]{1,0:T(8,128)}) custom-call(f32[16,256]{1,0:T(8,128)} %get-tuple-element.4.source, f32[2,256,128]{2,1,0:T(8,128)} %bitcast.2), custom_call_target="tpu_custom_call" | custom-call | tf_op jit(solution)/shard_map/hand_over/pallas_call | solution.py:432

commit v7 on v6

--- a/solution.py
+++ b/solution.py
@@ -160,12 +160,13 @@
         send_chunk(0, g)
         return 0
 
-    tables()
-    lax.fori_loop(0, 2, first_rows, 0)
+    lax.fori_loop(0, CHUNKS, first_rows, 0)
     pl.semaphore_wait(barrier, PLANE - 1 + NZ - 1)
     send_chunk(0, 0)
     send_chunk(0, 1)
-    lax.fori_loop(2, CHUNKS, first_rows_sent, 0)
+    send_chunk(0, 2)
+    send_chunk(0, 3)
+
 
     def scale_costs(r, _):
         for k in range(KK):
@@ -174,6 +175,7 @@
         return 0
 
     lax.fori_loop(0, ROWS, scale_costs, 0)
+    tables()
 
     def scale_turned(r, _):
         for k in range(KK):
@@ -313,13 +315,16 @@
                 gather(step, h)
 
                 def source_rows(g, _):
-                    source_half(g, h)
-                    if h == 1:
+                    if h == 0:
+                        source_half(2 * g, h)
+                        source_half(2 * g + 1, h)
+                    else:
+                        source_half(g, h)
                         keep_chunk(step, g, both_halves(g))
                         send_chunk(step, g)
                     return 0
 
-                lax.fori_loop(0, CHUNKS, source_rows, 0)
+                lax.fori_loop(0, CHUNKS if h else CHUNKS // 2, source_rows, 0)
 
         def target_rows_first(g, _):
             take_chunk(step, g + 1)
@@ -327,14 +332,15 @@
             return 0
 
         def target_rows_second(g, _):
-            target_part(g, (1,))
+            target_part(2 * g, (1,))
+            target_part(2 * g + 1, (1,))
             return 0
 
         take_chunk(step, 0)
         lax.fori_loop(0, CHUNKS - 1, target_rows_first, 0)
         target_part(CHUNKS - 1, (0,))
         scatter(step, 0)
-        lax.fori_loop(0, CHUNKS, target_rows_second, 0)
+        lax.fori_loop(0, CHUNKS // 2, target_rows_second, 0)
         scatter(step, 1)
         if step == 0:
             tlm_copy().wait()

time: 59.3 us -> 58.7 us (0.990)
  no operation moved by 1% of the time
where the time goes in v7:
time: 58.7 us; the launch traced here: 58.4 us
  Pallas kernels  57.8 us (98%)
  between operations  0.64 us (1%)
    pallas_call x1, Pallas kernels, per_device(): pl.pallas_call(body, name='sinkhorn', out_shape=(jax.ShapeDtypeStruct(sou...  56.1 us
    pallas_call x1, Pallas kernels, per_device(): pl.pallas_call(hand_over, name='hand_over', out_shape=(jax.ShapeDtypeStru...  1.67 us

profile of v7, /device:TPU:1, one launch (start us, length us, event | category | flops | bytes accessed | tf_op | source)
XLA Modules:
  0.0 58.4 jit_solution(17655844001036765675)
XLA Ops:
  0.6 56.1 %sinkhorn.1 = (f32[16,256]{1,0:T(8,128)}, f32[2,32,8,128]{3,2,1,0:T(8,128)}) custom-call(s32[2,16]{1,0:T(2,128)} %bitcast.3, bf16[16,2,256,256]{3,2,1,0:T(8,128)(2,1)} %cost_hbm.1, f32[16,256]{1,0:T(8,128)} %slm_ref.1, f32[256,256]{1,0:T(8,128)} %tlm_hbm.1), custom_call_target="tpu_custom_call" | custom-call | tf_op jit(solution)/shard_map/sinkhorn/pallas_call | solution.py:422
  56.8 1.7 %hand_over.1 = (f32[16,256]{1,0:T(8,128)}, f32[256,256]{1,0:T(8,128)}) custom-call(f32[16,256]{1,0:T(8,128)} %get-tuple-element.4.source, f32[2,256,128]{2,1,0:T(8,128)} %bitcast.2), custom_call_target="tpu_custom_call" | custom-call | tf_op jit(solution)/shard_map/hand_over/pallas_call | solution.py:438
